TPU v7x, 128 devices: a whole 4x4x4 slice. The times are simulated.
128 devices in a mesh: az: 32 (over y, x_hi, z), ax: 4 (over x_lo, core).
Axes of the slice: x: 4 (x_hi: 2, x_lo: 2; x = x_hi * 2 + x_lo), y: 4, z: 4, core: 2. Of those that a mesh axis runs over, the one named last changes fastest.
Arguments:
- start_field: float32 [16, 3, 64, 32, 512], P(None, None, 'az', 'ax'), may hold values from -4 to 4
- reluctivity: float32 [3, 64, 32, 512], P(None, 'az', 'ax'), may hold values from 0.05 to 1
- lamination: int32 [64, 32, 512], P('az', 'ax'), may hold values 0 or 1
- magnets: int32 [64, 32, 512], P('az', 'ax'), may hold values 0 or 1
- region_ids: int32 [64, 32, 512], P('az', 'ax'), may hold values from 0 to 127, as said below
- pieces: float32 [3, 16, 128], P(None, None, 'az'), may hold values from -5 to 5
- slot_map: int32 [16, 128], replicated, may hold values from 0 to 127, each once within a row
Outputs:
- solution_field: float32 [16, 3, 64, 32, 512], P(None, None, 'az', 'ax')
- residual: float32 [16, 3, 64, 32, 512], P(None, None, 'az', 'ax')
Inputs may be any that keep to these rules, and one draw needn't show every extreme that they name: `region_ids`: a cell of azimuthal sector s, the cells s * 2 to (s + 1) * 2 - 1 along the azimuth, holds a slot from s * 4 to (s + 1) * 4 - 1. `slot_map`: each row is a permutation.
All inputs are finite; a program needn't handle non-finite values. No bound on the sum of `lamination` or of `magnets` on one device may be relied on, other than what follows from the above.
Results may differ from a plain program's by a relative error of at most 0.00002.
Values sent between devices are 32-bit elements; how exact they have to be, the bound alone decides.
No kernel may reach another device: no remote copies, remote signals or barrier semaphores. Data moves between devices by JAX's collectives and lax.ppermute only.
A program may use at most 128 MiB of HBM per device.

v0:
```python
import jax
import jax.numpy as jnp
from jax import lax
from jax.sharding import PartitionSpec as P

mass_term = 1.0
cheb_centre = 8.5
cheb_halfwidth = 7.5
cheb_sigma = cheb_centre / cheb_halfwidth
rho_first = 1.0 / cheb_sigma
rho_second = 1.0 / (2.0 * cheb_sigma - rho_first)


def passed_along(value, axis, steps):
    count = lax.axis_size(axis)
    pairs = [(source, (source + steps) % count) for source in range(count)]
    return lax.ppermute(value, axis, pairs)


def from_behind(value, axis, steps):
    count = lax.axis_size(axis)
    first, last = (max(0, -steps), min(count, count - steps))
    return lax.ppermute(value, axis, [(source, source + steps) for source in range(first, last)])


def radial_forward(values):
    return jnp.concatenate([values[..., 1:], jnp.zeros_like(values[..., :1])], axis=-1) - values


def radial_backward(values):
    return values - jnp.concatenate([jnp.zeros_like(values[..., :1]), values[..., :-1]], axis=-1)


def curl_forward(core, along_a1, along_a2, along_z0, along_z2):
    return jnp.stack(
        [
            along_z2 - radial_forward(core[:, 1]),
            radial_forward(core[:, 0]) - along_a2,
            along_a1 - along_z0,
        ],
        axis=1,
    )


def curl_backward(core, along_a1, along_a2, along_z0, along_z2):
    return jnp.stack(
        [
            along_z2 - radial_backward(core[:, 1]),
            radial_backward(core[:, 0]) - along_a2,
            along_a1 - along_z0,
        ],
        axis=1,
    )


def residual_shifts(field, reluct, source):
    ahead_az = passed_along(field[:, 1:3, 0:1], "az", -1)
    ahead_ax = from_behind(jnp.stack([field[:, 0, :, 0:1], field[:, 2, :, 0:1]], axis=1), "ax", -1)
    step_az = jnp.concatenate([field[:, 1:3, 1:], ahead_az], axis=2) - field[:, 1:3]
    pair_field = jnp.stack([field[:, 0], field[:, 2]], axis=1)
    step_ax = jnp.concatenate([pair_field[:, :, :, 1:], ahead_ax], axis=3) - pair_field
    flux = curl_forward(field, step_az[:, 0], step_az[:, 1], step_ax[:, 0], step_ax[:, 1])
    intensity = reluct[None] * (flux - source)
    behind_az = passed_along(intensity[:, 1:3, -1:], "az", 1)
    behind_ax = from_behind(
        jnp.stack([intensity[:, 0, :, -1:], intensity[:, 2, :, -1:]], axis=1), "ax", 1
    )
    back_step_az = intensity[:, 1:3] - jnp.concatenate([behind_az, intensity[:, 1:3, :-1]], axis=2)
    pair_inten = jnp.stack([intensity[:, 0], intensity[:, 2]], axis=1)
    back_step_ax = pair_inten - jnp.concatenate([behind_ax, pair_inten[:, :, :, :-1]], axis=3)
    curl = curl_backward(
        intensity, back_step_az[:, 0], back_step_az[:, 1], back_step_ax[:, 0], back_step_ax[:, 1]
    )
    return -curl - mass_term * field


def shards(start_field, reluctivity, lamination, magnets, region_ids, pieces, slot_map):
    devs, comps, cells_az, cells_ax, radial = start_field.shape
    axial = jnp.array([0.0, 1.0, 0.0], jnp.float32)
    reluct = reluctivity * (
        1.0 + 3.0 * lamination.astype(jnp.float32)[None] * axial[:, None, None, None]
    )
    every_piece = lax.all_gather(pieces, "az", axis=2, tiled=True)
    slots_here = pieces.shape[2]
    base = lax.axis_index("az") * slots_here
    local_map = lax.dynamic_slice_in_dim(slot_map, base, slots_here, 1)
    local_table = jnp.take_along_axis(
        every_piece, jnp.broadcast_to(local_map[None], (comps, devs, slots_here)), axis=2
    )
    offset = (region_ids - base)[None, None]
    source = jnp.zeros(start_field.shape, jnp.float32)
    for slot in range(slots_here):
        values = jnp.transpose(local_table[:, :, slot])[:, :, None, None, None]
        source = jnp.where(offset == slot, values, source)
    source = source * magnets.astype(jnp.float32)[None, None]

    def residual_fn(field):
        return residual_shifts(field, reluct, source)

    first_res = residual_fn(start_field)
    first_dir = first_res / cheb_centre
    middle = start_field + first_dir
    second_res = residual_fn(middle)
    second_dir = rho_second * rho_first * first_dir + 2.0 * rho_second / cheb_halfwidth * second_res
    final = middle + second_dir
    return (final, residual_fn(final))


def solution(mesh):
    placed = (
        P(None, None, "az", "ax", None),
        P(None, "az", "ax", None),
        P("az", "ax", None),
        P("az", "ax", None),
        P("az", "ax", None),
        P(None, None, "az"),
        P(),
    )
    return jax.shard_map(
        shards,
        mesh=mesh,
        in_specs=placed,
        out_specs=(P(None, None, "az", "ax", None), P(None, None, "az", "ax", None)),
        check_vma=False,
    )
```

profile of v0, /device:TPU:1, one launch (start us, length us, event | category | flops | bytes accessed | tf_op | source)
XLA Modules:
  0.0 234.7 jit_solution(2493041710991904258)
XLA Ops:
  0.6 1.4 fusion.57
  2.8 3.3 %collective-permute-start = (f32[16,2,2,1,512]{4,3,2,0,1:T(1,128)}, f32[16,2,2,1,512]{4,3,2,0,1:T(1,128)S(1)}, u32[]{:S(2)}, u32[]{:S(2)}) collective-permute-start(f32[16,2,2,1,512]{4,3,2,0,1:T(1,128)} %pad_maximum_fusion.7), channel_id=1, source_target_pairs={{1,0},{2,1},{3,2},{5,4},{6,5},{7,6},{9,8},{10,9},{11,10},{13,12},{... | collective-permute-start | bytes 393224 | tf_op jit(solution)/shard_map/ppermute | solution.py:23
  6.1 2.3 fusion.56
  8.4 8.8 %collective-permute-start.1 = (f32[16,2,1,8,512]{4,3,2,0,1:T(8,128)}, f32[16,2,1,8,512]{4,3,2,0,1:T(8,128)}, u32[]{:S(2)}, u32[]{:S(2)}) collective-permute-start(f32[16,2,1,8,512]{4,3,2,0,1:T(8,128)} %get-tuple-element.77), channel_id=1, source_target_pairs={{0,124},{4,0},{8,4},{12,8},{16,12},{20,16},{24,20},{28,24},{32,28}... | collective-permute-start | bytes 1572872 | tf_op jit(solution)/shard_map/ppermute | solution.py:17
  18.2 85.1 %all_gather.3 = f32[3,16,128]{1,0,2:T(4,128)S(1)} all-gather(f32[3,16,4]{1,0,2:T(4,128)S(1)} %copy.91), channel_id=1, replica_groups=mesh['az'=32,'ax'=4] {'az'}, dimensions={2}, use_global_device_ids=true | all-gather | bytes 25344 | tf_op jit(solution)/shard_map/all_gather | solution.py:83
  105.4 2.1 gather_fusion
  110.2 1.2 slice.393
  112.9 1.3 slice_subtract_fusion.5
  116.0 15.4 %collective-permute-start.2 = (f32[16,2,2,1,512]{4,3,2,0,1:T(1,128)S(1)}, f32[16,2,2,1,512]{4,3,2,0,1:T(1,128)S(1)}, u32[]{:S(2)}, u32[]{:S(2)}) collective-permute-start(f32[16,2,2,1,512]{4,3,2,0,1:T(1,128)S(1)} %pad_maximum_fusion.8), channel_id=1, source_target_pairs={{0,1},{1,2},{2,3},{4,5},{5,6},{6,7},{8,9},{9,10},{10,11},{12,13},{... | collective-permute-start | bytes 393224 | tf_op jit(solution)/shard_map/ppermute | solution.py:23
  131.8 1.5 collective-permute-done.2
  133.7 16.4 %collective-permute-done.3 = f32[16,2,1,8,512]{4,3,2,0,1:T(8,128)S(1)} collective-permute-done((f32[16,2,1,8,512]{4,3,2,0,1:T(8,128)S(1)}, f32[16,2,1,8,512]{4,3,2,0,1:T(8,128)S(1)}, u32[]{:S(2)}, u32[]{:S(2)}) %collective-permute-start.3) | collective-permute-done | bytes 524320 | tf_op jit(solution)/shard_map/ppermute | solution.py:17
  151.5 1.9 collective-permute-start.4
  154.3 3.9 %collective-permute-done.4 = f32[16,2,2,1,512]{4,3,2,0,1:T(1,128)S(1)} collective-permute-done((f32[16,2,2,1,512]{4,3,2,0,1:T(1,128)S(1)}, f32[16,2,2,1,512]{4,3,2,0,1:T(1,128)S(1)}, u32[]{:S(2)}, u32[]{:S(2)}) %collective-permute-start.4) | collective-permute-done | bytes 131104 | tf_op jit(solution)/shard_map/ppermute | solution.py:23
  158.5 8.5 %collective-permute-done.5 = f32[16,2,1,8,512]{4,3,2,0,1:T(8,128)S(1)} collective-permute-done((f32[16,2,1,8,512]{4,3,2,0,1:T(8,128)S(1)}, f32[16,2,1,8,512]{4,3,2,0,1:T(8,128)S(1)}, u32[]{:S(2)}, u32[]{:S(2)}) %collective-permute-start.5) | collective-permute-done | bytes 524320 | tf_op jit(solution)/shard_map/ppermute | solution.py:17
  169.0 1.9 collective-permute-start.6
  171.5 1.4 collective-permute-done.6
  173.2 16.7 %collective-permute-done.7 = f32[16,2,1,8,512]{4,3,2,0,1:T(8,128)S(1)} collective-permute-done((f32[16,2,1,8,512]{4,3,2,0,1:T(8,128)S(1)}, f32[16,2,1,8,512]{4,3,2,0,1:T(8,128)S(1)}, u32[]{:S(2)}, u32[]{:S(2)}) %collective-permute-start.7) | collective-permute-done | bytes 524320 | tf_op jit(solution)/shard_map/ppermute | solution.py:17
  191.5 3.3 %collective-permute-start.8 = (f32[16,2,2,1,512]{4,3,2,0,1:T(1,128)S(1)}, f32[16,2,2,1,512]{4,3,2,0,1:T(1,128)S(1)}, u32[]{:S(2)}, u32[]{:S(2)}) collective-permute-start(f32[16,2,2,1,512]{4,3,2,0,1:T(1,128)S(1)} %pad_maximum_fusion.11), channel_id=1, source_target_pairs={{1,0},{2,1},{3,2},{5,4},{6,5},{7,6},{9,8},{10,9},{11,10},{13,12},{... | collective-permute-start | bytes 393224 | tf_op jit(solution)/shard_map/ppermute | solution.py:23
  195.7 2.4 %collective-permute-done.8 = f32[16,2,2,1,512]{4,3,2,0,1:T(1,128)S(1)} collective-permute-done((f32[16,2,2,1,512]{4,3,2,0,1:T(1,128)S(1)}, f32[16,2,2,1,512]{4,3,2,0,1:T(1,128)S(1)}, u32[]{:S(2)}, u32[]{:S(2)}) %collective-permute-start.8) | collective-permute-done | bytes 131104 | tf_op jit(solution)/shard_map/ppermute | solution.py:23
  198.3 10.1 %collective-permute-done.9 = f32[16,2,1,8,512]{4,3,2,0,1:T(8,128)S(1)} collective-permute-done((f32[16,2,1,8,512]{4,3,2,0,1:T(8,128)S(1)}, f32[16,2,1,8,512]{4,3,2,0,1:T(8,128)S(1)}, u32[]{:S(2)}, u32[]{:S(2)}) %collective-permute-start.9) | collective-permute-done | bytes 524320 | tf_op jit(solution)/shard_map/ppermute | solution.py:17
  210.5 1.9 collective-permute-start.10
  212.9 1.4 collective-permute-done.10
  214.7 16.5 %collective-permute-done.11 = f32[16,2,1,8,512]{4,3,2,0,1:T(8,128)S(1)} collective-permute-done((f32[16,2,1,8,512]{4,3,2,0,1:T(8,128)S(1)}, f32[16,2,1,8,512]{4,3,2,0,1:T(8,128)S(1)}, u32[]{:S(2)}, u32[]{:S(2)}) %collective-permute-start.11) | collective-permute-done | bytes 524320 | tf_op jit(solution)/shard_map/ppermute | solution.py:17
  231.9 2.8 %fusion.8 = (f32[16,3,2,8,512]{4,3,2,1,0:T(8,128)}, f32[16,3,2,8,512]{4,3,2,1,0:T(8,128)}) fusion(f32[16,1,2,8,512]{4,3,2,1,0:T(8,128)S(1)} %slice_subtract_fusion.6, f32[16,1,2,8,512]{4,3,2,1,0:T(8,128)S(1)} %get-tuple-element.21, f32[16,1,2,8,512]{4,3,2,1,0:T(8,128)S(1)} %get-tuple-element.20, f32[16,1,2,8,512]{4,3,2,0,1:T(8,128)S(1)} %slice_subtract_fusion.8, ...), kind=kLoop, calls=%fused_computation.15 | loop fusion | flops 7077888 | bytes 9437184 | tf_op jit(solution)/shard_map/sub | solution.py:74
  (98 shorter events, 22.1 us)
Async XLA Ops:
  0.6 16.5 %copy-start = (f32[16,3,2,8,512]{4,3,2,1,0:T(8,128)S(1)}, f32[16,3,2,8,512]{4,3,2,1,0:T(8,128)}, u32[]{:S(2)}) copy-start(f32[16,3,2,8,512]{4,3,2,1,0:T(8,128)} %param.8) | copy-start | bytes 4718596
  2.8 109.1 %collective-permute-start = (f32[16,2,2,1,512]{4,3,2,0,1:T(1,128)}, f32[16,2,2,1,512]{4,3,2,0,1:T(1,128)S(1)}, u32[]{:S(2)}, u32[]{:S(2)}) collective-permute-start(f32[16,2,2,1,512]{4,3,2,0,1:T(1,128)} %pad_maximum_fusion.7), channel_id=1, source_target_pairs={{1,0},{2,1},{3,2},{5,4},{6,5},{7,6},{9,8},{10,9},{11,10},{13,12},{... | collective-permute-start | bytes 393224 | tf_op jit(solution)/shard_map/ppermute | solution.py:23
  8.4 9.8 %copy-start.7 = (f32[3,16,4]{1,2,0:T(4,128)S(1)}, f32[3,16,4]{1,2,0:T(4,128)}, u32[]{:S(2)}) copy-start(f32[3,16,4]{1,2,0:T(4,128)} %param.13) | copy-start | bytes 2308
  8.4 94.9 %copy-start.6 = (s32[16,128]{1,0:T(8,128)S(1)}, s32[16,128]{1,0:T(8,128)}, u32[]{:S(2)}) copy-start(s32[16,128]{1,0:T(8,128)} %param.14) | copy-start | bytes 24580
  8.4 103.8 %collective-permute-start.1 = (f32[16,2,1,8,512]{4,3,2,0,1:T(8,128)}, f32[16,2,1,8,512]{4,3,2,0,1:T(8,128)}, u32[]{:S(2)}, u32[]{:S(2)}) collective-permute-start(f32[16,2,1,8,512]{4,3,2,0,1:T(8,128)} %get-tuple-element.77), channel_id=1, source_target_pairs={{0,124},{4,0},{8,4},{12,8},{16,12},{20,16},{24,20},{28,24},{32,28}... | collective-permute-start | bytes 1572872 | tf_op jit(solution)/shard_map/ppermute | solution.py:17
  103.4 0.6 copy-start.5
  103.4 0.6 copy-start.3
  107.6 4.0 %copy-start.4 = (s32[2,8,512]{2,1,0:T(8,128)S(1)}, s32[2,8,512]{2,1,0:T(8,128)}, u32[]{:S(2)}) copy-start(s32[2,8,512]{2,1,0:T(8,128)} %param.11) | copy-start | bytes 98308
  107.6 4.0 %copy-start.2 = (f32[3,2,8,512]{3,2,1,0:T(8,128)S(1)}, f32[3,2,8,512]{3,2,1,0:T(8,128)}, u32[]{:S(2)}) copy-start(f32[3,2,8,512]{3,2,1,0:T(8,128)} %param.9) | copy-start | bytes 294916
  107.6 4.0 %copy-start.8 = (f32[3]{0:T(128)S(1)}, f32[3]{0:T(128)}, u32[]{:S(2)}) copy-start(f32[3]{0:T(128)} %constant.50.clone) | copy-start | bytes 40
  111.9 1.0 copy-start.1
  116.0 17.4 %collective-permute-start.2 = (f32[16,2,2,1,512]{4,3,2,0,1:T(1,128)S(1)}, f32[16,2,2,1,512]{4,3,2,0,1:T(1,128)S(1)}, u32[]{:S(2)}, u32[]{:S(2)}) collective-permute-start(f32[16,2,2,1,512]{4,3,2,0,1:T(1,128)S(1)} %pad_maximum_fusion.8), channel_id=1, source_target_pairs={{0,1},{1,2},{2,3},{4,5},{5,6},{6,7},{8,9},{9,10},{10,11},{12,13},{... | collective-permute-start | bytes 393224 | tf_op jit(solution)/shard_map/ppermute | solution.py:23
  131.4 18.7 %collective-permute-start.3 = (f32[16,2,1,8,512]{4,3,2,0,1:T(8,128)S(1)}, f32[16,2,1,8,512]{4,3,2,0,1:T(8,128)S(1)}, u32[]{:S(2)}, u32[]{:S(2)}) collective-permute-start(f32[16,2,1,8,512]{4,3,2,0,1:T(8,128)S(1)} %get-tuple-element.66), channel_id=1, source_target_pairs={{0,4},{4,8},{8,12},{12,16},{16,20},{20,24},{24,28},{28,32},{32,36}... | collective-permute-start | bytes 1572872 | tf_op jit(solution)/shard_map/ppermute | solution.py:17
  151.5 6.7 %collective-permute-start.4 = (f32[16,2,2,1,512]{4,3,2,0,1:T(1,128)S(1)}, f32[16,2,2,1,512]{4,3,2,0,1:T(1,128)S(1)}, u32[]{:S(2)}, u32[]{:S(2)}) collective-permute-start(f32[16,2,2,1,512]{4,3,2,0,1:T(1,128)S(1)} %pad_maximum_fusion.9), channel_id=1, source_target_pairs={{1,0},{2,1},{3,2},{5,4},{6,5},{7,6},{9,8},{10,9},{11,10},{13,12},{... | collective-permute-start | bytes 393224 | tf_op jit(solution)/shard_map/ppermute | solution.py:23
  153.4 13.6 %collective-permute-start.5 = (f32[16,2,1,8,512]{4,3,2,0,1:T(8,128)S(1)}, f32[16,2,1,8,512]{4,3,2,0,1:T(8,128)S(1)}, u32[]{:S(2)}, u32[]{:S(2)}) collective-permute-start(f32[16,2,1,8,512]{4,3,2,0,1:T(8,128)S(1)} %get-tuple-element.57), channel_id=1, source_target_pairs={{0,124},{4,0},{8,4},{12,8},{16,12},{20,16},{24,20},{28,24},{32,28}... | collective-permute-start | bytes 1572872 | tf_op jit(solution)/shard_map/ppermute | solution.py:17
  169.0 3.9 %collective-permute-start.6 = (f32[16,2,2,1,512]{4,3,2,0,1:T(1,128)S(1)}, f32[16,2,2,1,512]{4,3,2,0,1:T(1,128)S(1)}, u32[]{:S(2)}, u32[]{:S(2)}) collective-permute-start(f32[16,2,2,1,512]{4,3,2,0,1:T(1,128)S(1)} %pad_maximum_fusion.10), channel_id=1, source_target_pairs={{0,1},{1,2},{2,3},{4,5},{5,6},{6,7},{8,9},{9,10},{10,11},{12,13},{... | collective-permute-start | bytes 393224 | tf_op jit(solution)/shard_map/ppermute | solution.py:23
  170.9 19.0 %collective-permute-start.7 = (f32[16,2,1,8,512]{4,3,2,0,1:T(8,128)S(1)}, f32[16,2,1,8,512]{4,3,2,0,1:T(8,128)S(1)}, u32[]{:S(2)}, u32[]{:S(2)}) collective-permute-start(f32[16,2,1,8,512]{4,3,2,0,1:T(8,128)S(1)} %get-tuple-element.46), channel_id=1, source_target_pairs={{0,4},{4,8},{8,12},{12,16},{16,20},{20,24},{24,28},{28,32},{32,36}... | collective-permute-start | bytes 1572872 | tf_op jit(solution)/shard_map/ppermute | solution.py:17
  191.5 6.6 %collective-permute-start.8 = (f32[16,2,2,1,512]{4,3,2,0,1:T(1,128)S(1)}, f32[16,2,2,1,512]{4,3,2,0,1:T(1,128)S(1)}, u32[]{:S(2)}, u32[]{:S(2)}) collective-permute-start(f32[16,2,2,1,512]{4,3,2,0,1:T(1,128)S(1)} %pad_maximum_fusion.11), channel_id=1, source_target_pairs={{1,0},{2,1},{3,2},{5,4},{6,5},{7,6},{9,8},{10,9},{11,10},{13,12},{... | collective-permute-start | bytes 393224 | tf_op jit(solution)/shard_map/ppermute | solution.py:23
  194.7 13.7 %collective-permute-start.9 = (f32[16,2,1,8,512]{4,3,2,0,1:T(8,128)S(1)}, f32[16,2,1,8,512]{4,3,2,0,1:T(8,128)S(1)}, u32[]{:S(2)}, u32[]{:S(2)}) collective-permute-start(f32[16,2,1,8,512]{4,3,2,0,1:T(8,128)S(1)} %get-tuple-element.37), channel_id=1, source_target_pairs={{0,124},{4,0},{8,4},{12,8},{16,12},{20,16},{24,20},{28,24},{32,28}... | collective-permute-start | bytes 1572872 | tf_op jit(solution)/shard_map/ppermute | solution.py:17
  210.5 3.9 %collective-permute-start.10 = (f32[16,2,2,1,512]{4,3,2,0,1:T(1,128)S(1)}, f32[16,2,2,1,512]{4,3,2,0,1:T(1,128)S(1)}, u32[]{:S(2)}, u32[]{:S(2)}) collective-permute-start(f32[16,2,2,1,512]{4,3,2,0,1:T(1,128)S(1)} %pad_maximum_fusion.12), channel_id=1, source_target_pairs={{0,1},{1,2},{2,3},{4,5},{5,6},{6,7},{8,9},{9,10},{10,11},{12,13},{... | collective-permute-start | bytes 393224 | tf_op jit(solution)/shard_map/ppermute | solution.py:23
  212.4 18.8 %collective-permute-start.11 = (f32[16,2,1,8,512]{4,3,2,0,1:T(8,128)S(1)}, f32[16,2,1,8,512]{4,3,2,0,1:T(8,128)S(1)}, u32[]{:S(2)}, u32[]{:S(2)}) collective-permute-start(f32[16,2,1,8,512]{4,3,2,0,1:T(8,128)S(1)} %get-tuple-element.26), channel_id=1, source_target_pairs={{0,4},{4,8},{8,12},{12,16},{16,20},{20,24},{24,28},{28,32},{32,36}... | collective-permute-start | bytes 1572872 | tf_op jit(solution)/shard_map/ppermute | solution.py:17
where the time goes:
time: 235 us
  blocking collectives  85.1 us (36%)
  waiting for transfers between devices  78.6 us (33%)
  starting transfers between devices  37.1 us (16%)
  other arithmetic  19 us (8%)
  local copies, waits for them, and re-layouts  13.7 us (6%)
    all_gather x1, blocking collectives, shards(): every_piece = lax.all_gather(pieces, 'az', axis=2, tiled=True)  85.1 us
    ppermute x6, waiting for transfers between devices, passed_along(): return lax.ppermute(value, axis, pairs)  68.1 us
    ppermute x6, starting transfers between devices, from_behind(): lax.ppermute(value, axis, [(source, source + steps) for source in range(f...  27.8 us
    ppermute x6, waiting for transfers between devices, from_behind(): lax.ppermute(value, axis, [(source, source + steps) for source in range(f...  10.5 us
    ppermute x6, starting transfers between devices, passed_along(): return lax.ppermute(value, axis, pairs)  9.31 us
  transfers between devices with their start and end apart: 12, of which 10 were waited for; matrix products, arithmetic and copies ran while one was open for 7% of the time, Pallas kernels for 0%

commit v1 on v0

--- a/solution.py
+++ b/solution.py
@@ -80,7 +80,9 @@
     reluct = reluctivity * (
         1.0 + 3.0 * lamination.astype(jnp.float32)[None] * axial[:, None, None, None]
     )
-    every_piece = lax.all_gather(pieces, "az", axis=2, tiled=True)
+    every_piece = jnp.concatenate(
+        lax.all_to_all(jnp.stack([pieces] * lax.axis_size("az")), "az", 0, 0), axis=2
+    )
     slots_here = pieces.shape[2]
     base = lax.axis_index("az") * slots_here
     local_map = lax.dynamic_slice_in_dim(slot_map, base, slots_here, 1)

time: 235 us -> 150 us (0.64)
  blocking collectives: 85.1 us -> 0 us
  starting transfers between devices: 37.1 us -> 29.4 us
  waiting for transfers between devices: 78.6 us -> 82.3 us
  local copies, waits for them, and re-layouts: 13.7 us -> 16.1 us
    all_gather x1 -> x0, blocking collectives: 85.1 us -> none  [shards(): every_piece = lax.all_gather(pieces, 'az', axis=2, tiled=True)]
    ppermute x6, starting transfers between devices: 27.8 us -> 15.2 us  [from_behind(): lax.ppermute(value, axis, [(source, source + steps) for source in range(f...]
    all_to_all x0 -> x1, starting transfers between devices: none -> 4.52 us  [shards(): lax.all_to_all(jnp.stack([pieces] * lax.axis_size('az')), 'az', 0, 0)]
  transfers between devices with their start and end apart: 12 -> 13, of which waited for: 10 -> 11; matrix products, arithmetic and copies ran while one was open for 7% -> 13% of each run, Pallas kernels for 0% -> 0%
where the time goes in v1:
time: 150 us
  waiting for transfers between devices  82.3 us (55%)
  starting transfers between devices  29.4 us (20%)
  other arithmetic  20.5 us (14%)
  local copies, waits for them, and re-layouts  16.1 us (11%)
    ppermute x6, waiting for transfers between devices, passed_along(): return lax.ppermute(value, axis, pairs)  68.6 us
    ppermute x6, starting transfers between devices, from_behind(): lax.ppermute(value, axis, [(source, source + steps) for source in range(f...  15.2 us
    ppermute x6, waiting for transfers between devices, from_behind(): lax.ppermute(value, axis, [(source, source + steps) for source in range(f...  12.4 us
    ppermute x6, starting transfers between devices, passed_along(): return lax.ppermute(value, axis, pairs)  9.72 us
    all_to_all x1, starting transfers between devices, shards(): lax.all_to_all(jnp.stack([pieces] * lax.axis_size('az')), 'az', 0, 0)  4.52 us
  transfers between devices with their start and end apart: 13, of which 11 were waited for; matrix products, arithmetic and copies ran while one was open for 13% of the time, Pallas kernels for 0%

profile of v1, /device:TPU:1, one launch (start us, length us, event | category | flops | bytes accessed | tf_op | source)
XLA Modules:
  0.0 149.7 jit_solution(14004805324984308221)
XLA Ops:
  0.7 1.4 fusion.57
  2.2 3.3 %collective-permute-start = (f32[16,2,2,1,512]{4,3,2,0,1:T(1,128)S(1)}, f32[16,2,2,1,512]{4,3,2,0,1:T(1,128)S(1)}, u32[]{:S(2)}, u32[]{:S(2)}) collective-permute-start(f32[16,2,2,1,512]{4,3,2,0,1:T(1,128)S(1)} %pad_maximum_fusion.7), channel_id=1, source_target_pairs={{1,0},{2,1},{3,2},{5,4},{6,5},{7,6},{9,8},{10,9},{11,10},{13,12},{... | collective-permute-start | bytes 393224 | tf_op jit(solution)/shard_map/ppermute | solution.py:23
  5.5 2.3 %fusion.56 = (f32[16,2,1,8,512]{4,3,2,0,1:T(8,128)}, f32[16,2,1,8,512]{4,3,2,0,1:T(8,128)}) fusion(f32[16,3,2,8,512]{4,3,2,1,0:T(8,128)} %param.8), kind=kLoop, calls=%fused_computation.144 | loop fusion | bytes 2097152 | tf_op jit(solution)/shard_map/slice | solution.py:59
  7.8 8.8 %collective-permute-start.1 = (f32[16,2,1,8,512]{4,3,2,0,1:T(8,128)}, f32[16,2,1,8,512]{4,3,2,0,1:T(8,128)}, u32[]{:S(2)}, u32[]{:S(2)}) collective-permute-start(f32[16,2,1,8,512]{4,3,2,0,1:T(8,128)} %get-tuple-element.75), channel_id=1, source_target_pairs={{0,124},{4,0},{8,4},{12,8},{16,12},{20,16},{24,20},{28,24},{32,28}... | collective-permute-start | bytes 1572872 | tf_op jit(solution)/shard_map/ppermute | solution.py:17
  17.4 4.5 %all-to-all-start = ((f32[32,1,192]{2,1,0:T(1,128)}), f32[32,1,192]{2,1,0:T(1,128)}, u32[]{:S(2)}, u32[]{:S(2)}) async-start(f32[32,1,192]{2,1,0:T(1,128)} %reshape.51), calls=%async_computation | async-start | bytes 65536 | tf_op jit(solution)/shard_map/all_to_all | solution.py:84
  29.3 1.4 all-to-all-done
  31.2 1.4 reduce.8
  32.8 2.0 %gather_fusion = f32[192]{0:T(256)S(1)} fusion(f32[3,16,128]{1,2,0:T(8,128)S(1)} %bitcast.167, s32[192]{0:T(256)S(1)} %reshape.41), kind=kCustom, calls=%fused_computation | custom fusion | bytes 3840 | tf_op jit(solution)/shard_map/jit(take_along_axis)/gather | solution.py:89
  35.1 1.6 %fusion.19 = f32[16,2,2,8,512]{4,3,2,0,1:T(8,128)S(1)} fusion(f32[16,1,2,8,512]{4,3,2,0,1:T(8,128)S(1)} %get-tuple-element.72, f32[16,1,2,8,512]{4,3,2,0,1:T(8,128)S(1)} %get-tuple-element.73, f32[16,2,2,1,512]{4,3,2,0,1:T(1,128)S(1)} %collective-permute-done, f32[16,2,2,7,512]{4,3,2,0,1:T(8,128)} %fusion.18), kind=kLoop, calls=%fused_computation.46 | loop fusion | flops 786432 | bytes 3145728 | tf_op jit(solution)/shard_map/sub | solution.py:61
  40.9 3.8 %collective-permute-start.2 = (f32[16,2,2,1,512]{4,3,2,0,1:T(1,128)S(1)}, f32[16,2,2,1,512]{4,3,2,0,1:T(1,128)S(1)}, u32[]{:S(2)}, u32[]{:S(2)}) collective-permute-start(f32[16,2,2,1,512]{4,3,2,0,1:T(1,128)S(1)} %pad_maximum_fusion.8), channel_id=1, source_target_pairs={{0,1},{1,2},{2,3},{4,5},{5,6},{6,7},{8,9},{9,10},{10,11},{12,13},{... | collective-permute-start | bytes 393224 | tf_op jit(solution)/shard_map/ppermute | solution.py:23
  46.9 17.0 %collective-permute-done.3 = f32[16,2,1,8,512]{4,3,2,0,1:T(8,128)S(1)} collective-permute-done((f32[16,2,1,8,512]{4,3,2,0,1:T(8,128)S(1)}, f32[16,2,1,8,512]{4,3,2,0,1:T(8,128)S(1)}, u32[]{:S(2)}, u32[]{:S(2)}) %collective-permute-start.3) | collective-permute-done | bytes 524320 | tf_op jit(solution)/shard_map/ppermute | solution.py:17
  65.3 1.9 %collective-permute-start.4 = (f32[16,2,2,1,512]{4,3,2,0,1:T(1,128)S(1)}, f32[16,2,2,1,512]{4,3,2,0,1:T(1,128)S(1)}, u32[]{:S(2)}, u32[]{:S(2)}) collective-permute-start(f32[16,2,2,1,512]{4,3,2,0,1:T(1,128)S(1)} %pad_maximum_fusion.9), channel_id=1, source_target_pairs={{1,0},{2,1},{3,2},{5,4},{6,5},{7,6},{9,8},{10,9},{11,10},{13,12},{... | collective-permute-start | bytes 393224 | tf_op jit(solution)/shard_map/ppermute | solution.py:23
  68.2 5.2 %collective-permute-done.4 = f32[16,2,2,1,512]{4,3,2,0,1:T(1,128)S(1)} collective-permute-done((f32[16,2,2,1,512]{4,3,2,0,1:T(1,128)S(1)}, f32[16,2,2,1,512]{4,3,2,0,1:T(1,128)S(1)}, u32[]{:S(2)}, u32[]{:S(2)}) %collective-permute-start.4) | collective-permute-done | bytes 131104 | tf_op jit(solution)/shard_map/ppermute | solution.py:23
  73.7 7.2 %collective-permute-done.5 = f32[16,2,1,8,512]{4,3,2,0,1:T(8,128)S(1)} collective-permute-done((f32[16,2,1,8,512]{4,3,2,0,1:T(8,128)S(1)}, f32[16,2,1,8,512]{4,3,2,0,1:T(8,128)S(1)}, u32[]{:S(2)}, u32[]{:S(2)}) %collective-permute-start.5) | collective-permute-done | bytes 524320 | tf_op jit(solution)/shard_map/ppermute | solution.py:17
  82.9 1.9 %collective-permute-start.6 = (f32[16,2,2,1,512]{4,3,2,0,1:T(1,128)S(1)}, f32[16,2,2,1,512]{4,3,2,0,1:T(1,128)S(1)}, u32[]{:S(2)}, u32[]{:S(2)}) collective-permute-start(f32[16,2,2,1,512]{4,3,2,0,1:T(1,128)S(1)} %pad_maximum_fusion.10), channel_id=1, source_target_pairs={{0,1},{1,2},{2,3},{4,5},{5,6},{6,7},{8,9},{9,10},{10,11},{12,13},{... | collective-permute-start | bytes 393224 | tf_op jit(solution)/shard_map/ppermute | solution.py:23
  85.5 1.3 collective-permute-done.6
  87.1 18.7 %collective-permute-done.7 = f32[16,2,1,8,512]{4,3,2,0,1:T(8,128)S(1)} collective-permute-done((f32[16,2,1,8,512]{4,3,2,0,1:T(8,128)S(1)}, f32[16,2,1,8,512]{4,3,2,0,1:T(8,128)S(1)}, u32[]{:S(2)}, u32[]{:S(2)}) %collective-permute-start.7) | collective-permute-done | bytes 524320 | tf_op jit(solution)/shard_map/ppermute | solution.py:17
  107.4 2.3 %collective-permute-start.8 = (f32[16,2,2,1,512]{4,3,2,0,1:T(1,128)S(1)}, f32[16,2,2,1,512]{4,3,2,0,1:T(1,128)S(1)}, u32[]{:S(2)}, u32[]{:S(2)}) collective-permute-start(f32[16,2,2,1,512]{4,3,2,0,1:T(1,128)S(1)} %pad_maximum_fusion.11), channel_id=1, source_target_pairs={{1,0},{2,1},{3,2},{5,4},{6,5},{7,6},{9,8},{10,9},{11,10},{13,12},{... | collective-permute-start | bytes 393224 | tf_op jit(solution)/shard_map/ppermute | solution.py:23
  110.7 3.3 %collective-permute-done.8 = f32[16,2,2,1,512]{4,3,2,0,1:T(1,128)S(1)} collective-permute-done((f32[16,2,2,1,512]{4,3,2,0,1:T(1,128)S(1)}, f32[16,2,2,1,512]{4,3,2,0,1:T(1,128)S(1)}, u32[]{:S(2)}, u32[]{:S(2)}) %collective-permute-start.8) | collective-permute-done | bytes 131104 | tf_op jit(solution)/shard_map/ppermute | solution.py:23
  114.4 9.1 %collective-permute-done.9 = f32[16,2,1,8,512]{4,3,2,0,1:T(8,128)S(1)} collective-permute-done((f32[16,2,1,8,512]{4,3,2,0,1:T(8,128)S(1)}, f32[16,2,1,8,512]{4,3,2,0,1:T(8,128)S(1)}, u32[]{:S(2)}, u32[]{:S(2)}) %collective-permute-start.9) | collective-permute-done | bytes 524320 | tf_op jit(solution)/shard_map/ppermute | solution.py:17
  125.4 1.9 %collective-permute-start.10 = (f32[16,2,2,1,512]{4,3,2,0,1:T(1,128)S(1)}, f32[16,2,2,1,512]{4,3,2,0,1:T(1,128)S(1)}, u32[]{:S(2)}, u32[]{:S(2)}) collective-permute-start(f32[16,2,2,1,512]{4,3,2,0,1:T(1,128)S(1)} %pad_maximum_fusion.12), channel_id=1, source_target_pairs={{0,1},{1,2},{2,3},{4,5},{5,6},{6,7},{8,9},{9,10},{10,11},{12,13},{... | collective-permute-start | bytes 393224 | tf_op jit(solution)/shard_map/ppermute | solution.py:23
  127.8 1.5 %collective-permute-done.10 = f32[16,2,2,1,512]{4,3,2,0,1:T(1,128)S(1)} collective-permute-done((f32[16,2,2,1,512]{4,3,2,0,1:T(1,128)S(1)}, f32[16,2,2,1,512]{4,3,2,0,1:T(1,128)S(1)}, u32[]{:S(2)}, u32[]{:S(2)}) %collective-permute-start.10) | collective-permute-done | bytes 131104 | tf_op jit(solution)/shard_map/ppermute | solution.py:23
  129.6 16.6 %collective-permute-done.11 = f32[16,2,1,8,512]{4,3,2,0,1:T(8,128)S(1)} collective-permute-done((f32[16,2,1,8,512]{4,3,2,0,1:T(8,128)S(1)}, f32[16,2,1,8,512]{4,3,2,0,1:T(8,128)S(1)}, u32[]{:S(2)}, u32[]{:S(2)}) %collective-permute-start.11) | collective-permute-done | bytes 524320 | tf_op jit(solution)/shard_map/ppermute | solution.py:17
  146.9 2.8 %fusion.8 = (f32[16,3,2,8,512]{4,3,2,1,0:T(8,128)}, f32[16,3,2,8,512]{4,3,2,1,0:T(8,128)}) fusion(f32[16,1,2,8,512]{4,3,2,1,0:T(8,128)S(1)} %slice_subtract_fusion.6, f32[16,1,2,8,512]{4,3,2,1,0:T(8,128)S(1)} %get-tuple-element.19, f32[16,1,2,8,512]{4,3,2,1,0:T(8,128)S(1)} %get-tuple-element.18, f32[16,1,2,8,512]{4,3,2,0,1:T(8,128)S(1)} %slice_subtract_fusion.8, ...), kind=kLoop, calls=%fused_computation.15 | loop fusion | flops 7077888 | bytes 9437184 | tf_op jit(solution)/shard_map/sub | solution.py:74
  (117 shorter events, 27.2 us)
Async XLA Ops:
  0.6 15.9 %copy-start = (f32[3,16,4]{1,2,0:T(4,128)S(1)}, f32[3,16,4]{1,2,0:T(4,128)}, u32[]{:S(2)}) copy-start(f32[3,16,4]{1,2,0:T(4,128)} %param.13) | copy-start | bytes 2308
  0.6 21.3 %copy-start.2 = (f32[16,3,2,8,512]{4,3,2,1,0:T(8,128)S(1)}, f32[16,3,2,8,512]{4,3,2,1,0:T(8,128)}, u32[]{:S(2)}) copy-start(f32[16,3,2,8,512]{4,3,2,1,0:T(8,128)} %param.8) | copy-start | bytes 4718596
  2.2 33.0 %collective-permute-start = (f32[16,2,2,1,512]{4,3,2,0,1:T(1,128)S(1)}, f32[16,2,2,1,512]{4,3,2,0,1:T(1,128)S(1)}, u32[]{:S(2)}, u32[]{:S(2)}) collective-permute-start(f32[16,2,2,1,512]{4,3,2,0,1:T(1,128)S(1)} %pad_maximum_fusion.7), channel_id=1, source_target_pairs={{1,0},{2,1},{3,2},{5,4},{6,5},{7,6},{9,8},{10,9},{11,10},{13,12},{... | collective-permute-start | bytes 393224 | tf_op jit(solution)/shard_map/ppermute | solution.py:23
  7.8 28.9 %collective-permute-start.1 = (f32[16,2,1,8,512]{4,3,2,0,1:T(8,128)}, f32[16,2,1,8,512]{4,3,2,0,1:T(8,128)}, u32[]{:S(2)}, u32[]{:S(2)}) collective-permute-start(f32[16,2,1,8,512]{4,3,2,0,1:T(8,128)} %get-tuple-element.75), channel_id=1, source_target_pairs={{0,124},{4,0},{8,4},{12,8},{16,12},{20,16},{24,20},{28,24},{32,28}... | collective-permute-start | bytes 1572872 | tf_op jit(solution)/shard_map/ppermute | solution.py:17
  17.4 13.3 %all-to-all-start = ((f32[32,1,192]{2,1,0:T(1,128)}), f32[32,1,192]{2,1,0:T(1,128)}, u32[]{:S(2)}, u32[]{:S(2)}) async-start(f32[32,1,192]{2,1,0:T(1,128)} %reshape.51), calls=%async_computation | async-start | bytes 65536 | tf_op jit(solution)/shard_map/all_to_all | solution.py:84
  21.9 1.2 copy-start.9
  22.0 1.2 copy-start.10
  23.1 3.4 %copy-start.3 = (f32[16,2,8,512]{3,2,1,0:T(8,128)S(1)}, f32[16,2,8,512]{3,2,1,0:T(8,128)}, u32[]{:S(2)}) copy-start(f32[16,2,8,512]{3,2,1,0:T(8,128)} %get-tuple-element.70) | copy-start | bytes 1572868
  23.2 4.3 %copy-start.7 = (s32[16,4]{1,0:T(8,128)}, s32[16,4]{1,0:T(8,128)S(1)}, u32[]{:S(2)}) copy-start(s32[16,4]{1,0:T(8,128)S(1)} %broadcast_add_fusion) | copy-start | bytes 772
  26.4 2.0 %copy-start.11 = (s32[2,8,512]{2,1,0:T(8,128)S(1)}, s32[2,8,512]{2,1,0:T(8,128)}, u32[]{:S(2)}) copy-start(s32[2,8,512]{2,1,0:T(8,128)} %param.11) | copy-start | bytes 98308
  32.8 2.1 %copy-start.8 = (s32[16,4]{1,0:T(8,128)S(1)}, s32[16,4]{1,0:T(8,128)}, u32[]{:S(2)}) copy-start(s32[16,4]{1,0:T(8,128)} %copy-done.7) | copy-start | bytes 772
  32.8 2.1 %copy-start.13 = (pred[16,4]{1,0:T(8,128)(4,1)S(1)}, pred[16,4]{1,0:T(8,128)(4,1)}, u32[]{:S(2)}) copy-start(pred[16,4]{1,0:T(8,128)(4,1)} %copy-done.12) | copy-start | bytes 196
  35.1 1.6 %copy-start.4 = (f32[16,2,1,8,512]{4,3,2,0,1:T(8,128)S(1)}, f32[16,2,1,8,512]{4,3,2,0,1:T(8,128)}, u32[]{:S(2)}) copy-start(f32[16,2,1,8,512]{4,3,2,0,1:T(8,128)} %get-tuple-element.74) | copy-start | bytes 1572868
  40.9 5.7 %collective-permute-start.2 = (f32[16,2,2,1,512]{4,3,2,0,1:T(1,128)S(1)}, f32[16,2,2,1,512]{4,3,2,0,1:T(1,128)S(1)}, u32[]{:S(2)}, u32[]{:S(2)}) collective-permute-start(f32[16,2,2,1,512]{4,3,2,0,1:T(1,128)S(1)} %pad_maximum_fusion.8), channel_id=1, source_target_pairs={{0,1},{1,2},{2,3},{4,5},{5,6},{6,7},{8,9},{9,10},{10,11},{12,13},{... | collective-permute-start | bytes 393224 | tf_op jit(solution)/shard_map/ppermute | solution.py:23
  44.7 19.2 %collective-permute-start.3 = (f32[16,2,1,8,512]{4,3,2,0,1:T(8,128)S(1)}, f32[16,2,1,8,512]{4,3,2,0,1:T(8,128)S(1)}, u32[]{:S(2)}, u32[]{:S(2)}) collective-permute-start(f32[16,2,1,8,512]{4,3,2,0,1:T(8,128)S(1)} %get-tuple-element.64), channel_id=1, source_target_pairs={{0,4},{4,8},{8,12},{12,16},{16,20},{20,24},{24,28},{28,32},{32,36}... | collective-permute-start | bytes 1572872 | tf_op jit(solution)/shard_map/ppermute | solution.py:17
  65.3 8.1 %collective-permute-start.4 = (f32[16,2,2,1,512]{4,3,2,0,1:T(1,128)S(1)}, f32[16,2,2,1,512]{4,3,2,0,1:T(1,128)S(1)}, u32[]{:S(2)}, u32[]{:S(2)}) collective-permute-start(f32[16,2,2,1,512]{4,3,2,0,1:T(1,128)S(1)} %pad_maximum_fusion.9), channel_id=1, source_target_pairs={{1,0},{2,1},{3,2},{5,4},{6,5},{7,6},{9,8},{10,9},{11,10},{13,12},{... | collective-permute-start | bytes 393224 | tf_op jit(solution)/shard_map/ppermute | solution.py:23
  67.3 13.6 %collective-permute-start.5 = (f32[16,2,1,8,512]{4,3,2,0,1:T(8,128)S(1)}, f32[16,2,1,8,512]{4,3,2,0,1:T(8,128)S(1)}, u32[]{:S(2)}, u32[]{:S(2)}) collective-permute-start(f32[16,2,1,8,512]{4,3,2,0,1:T(8,128)S(1)} %get-tuple-element.55), channel_id=1, source_target_pairs={{0,124},{4,0},{8,4},{12,8},{16,12},{20,16},{24,20},{28,24},{32,28}... | collective-permute-start | bytes 1572872 | tf_op jit(solution)/shard_map/ppermute | solution.py:17
  82.9 3.9 %collective-permute-start.6 = (f32[16,2,2,1,512]{4,3,2,0,1:T(1,128)S(1)}, f32[16,2,2,1,512]{4,3,2,0,1:T(1,128)S(1)}, u32[]{:S(2)}, u32[]{:S(2)}) collective-permute-start(f32[16,2,2,1,512]{4,3,2,0,1:T(1,128)S(1)} %pad_maximum_fusion.10), channel_id=1, source_target_pairs={{0,1},{1,2},{2,3},{4,5},{5,6},{6,7},{8,9},{9,10},{10,11},{12,13},{... | collective-permute-start | bytes 393224 | tf_op jit(solution)/shard_map/ppermute | solution.py:23
  84.9 20.9 %collective-permute-start.7 = (f32[16,2,1,8,512]{4,3,2,0,1:T(8,128)S(1)}, f32[16,2,1,8,512]{4,3,2,0,1:T(8,128)S(1)}, u32[]{:S(2)}, u32[]{:S(2)}) collective-permute-start(f32[16,2,1,8,512]{4,3,2,0,1:T(8,128)S(1)} %get-tuple-element.44), channel_id=1, source_target_pairs={{0,4},{4,8},{8,12},{12,16},{16,20},{20,24},{24,28},{28,32},{32,36}... | collective-permute-start | bytes 1572872 | tf_op jit(solution)/shard_map/ppermute | solution.py:17
  107.4 6.6 %collective-permute-start.8 = (f32[16,2,2,1,512]{4,3,2,0,1:T(1,128)S(1)}, f32[16,2,2,1,512]{4,3,2,0,1:T(1,128)S(1)}, u32[]{:S(2)}, u32[]{:S(2)}) collective-permute-start(f32[16,2,2,1,512]{4,3,2,0,1:T(1,128)S(1)} %pad_maximum_fusion.11), channel_id=1, source_target_pairs={{1,0},{2,1},{3,2},{5,4},{6,5},{7,6},{9,8},{10,9},{11,10},{13,12},{... | collective-permute-start | bytes 393224 | tf_op jit(solution)/shard_map/ppermute | solution.py:23
  109.7 13.7 %collective-permute-start.9 = (f32[16,2,1,8,512]{4,3,2,0,1:T(8,128)S(1)}, f32[16,2,1,8,512]{4,3,2,0,1:T(8,128)S(1)}, u32[]{:S(2)}, u32[]{:S(2)}) collective-permute-start(f32[16,2,1,8,512]{4,3,2,0,1:T(8,128)S(1)} %get-tuple-element.35), channel_id=1, source_target_pairs={{0,124},{4,0},{8,4},{12,8},{16,12},{20,16},{24,20},{28,24},{32,28}... | collective-permute-start | bytes 1572872 | tf_op jit(solution)/shard_map/ppermute | solution.py:17
  125.4 3.9 %collective-permute-start.10 = (f32[16,2,2,1,512]{4,3,2,0,1:T(1,128)S(1)}, f32[16,2,2,1,512]{4,3,2,0,1:T(1,128)S(1)}, u32[]{:S(2)}, u32[]{:S(2)}) collective-permute-start(f32[16,2,2,1,512]{4,3,2,0,1:T(1,128)S(1)} %pad_maximum_fusion.12), channel_id=1, source_target_pairs={{0,1},{1,2},{2,3},{4,5},{5,6},{6,7},{8,9},{9,10},{10,11},{12,13},{... | collective-permute-start | bytes 393224 | tf_op jit(solution)/shard_map/ppermute | solution.py:23
  127.4 18.8 %collective-permute-start.11 = (f32[16,2,1,8,512]{4,3,2,0,1:T(8,128)S(1)}, f32[16,2,1,8,512]{4,3,2,0,1:T(8,128)S(1)}, u32[]{:S(2)}, u32[]{:S(2)}) collective-permute-start(f32[16,2,1,8,512]{4,3,2,0,1:T(8,128)S(1)} %get-tuple-element.24), channel_id=1, source_target_pairs={{0,4},{4,8},{8,12},{12,16},{16,20},{20,24},{24,28},{28,32},{32,36}... | collective-permute-start | bytes 1572872 | tf_op jit(solution)/shard_map/ppermute | solution.py:17
  146.9 2.8 %copy-start.1 = (f32[3,16,4]{1,2,0:T(4,128)S(1)}, f32[3,16,4]{1,2,0:T(4,128)}, u32[]{:S(2)}) copy-start(f32[3,16,4]{1,2,0:T(4,128)} %param.13) | copy-start | bytes 2308
  (4 other events, 3.9 us)
